TPU v7x, 512 devices: a whole 4x8x8 slice. The times are simulated.
512 devices in a mesh: ctx: 64 (over z, x, core), tp: 8 (over y).
Axes of the slice: x: 4, y: 8, z: 8, core: 2. Of those that a mesh axis runs over, the one named last changes fastest.
Arguments:
- queries: bfloat16 [32768, 4096], P('ctx', 'tp'), may hold values from -6 to 6
- keys: bfloat16 [32768, 4096], P('ctx', 'tp'), may hold values from -6 to 6
- values: bfloat16 [32768, 4096], P('ctx', 'tp'), may hold values from -6 to 6
- out_weight: bfloat16 [4096, 4096], P('tp', 'ctx'), may hold values from -0.09375 to 0.09375
Outputs:
- mixed: bfloat16 [32768, 4096], P(('ctx', 'tp'))
All inputs are finite; a program needn't handle non-finite values.
Results may differ from a plain program's by a relative error of at most 0.018.
Values may be sent and summed in bfloat16 or wider, within the bound.
No kernel may reach another device: no remote copies, remote signals or barrier semaphores. Data moves between devices by JAX's collectives and lax.ppermute only.
A program may use at most 64 MiB of HBM per device.

v0:
```python
import jax
import jax.numpy as jnp
from jax import lax
from jax.sharding import PartitionSpec as P

HD = 128


def prefix(part, axis, combine, identity):
    place = lax.axis_index(axis)
    gathered = lax.all_gather(part, axis)
    state = jnp.zeros_like(part) + jnp.asarray(identity, part.dtype)

    def one(step, state):
        return combine(state, lax.dynamic_index_in_dim(gathered, step, 0, False))

    return lax.fori_loop(0, place, one, state)


def add_states(earlier, later):
    return earlier + later


def on_device(queries, keys, values, out_weight):
    tok_rows = queries.shape[0]
    head_dim = HD
    heads_here = queries.shape[1] // head_dim
    block_len = min(tok_rows, 512)
    blocks = tok_rows // block_len
    shape = (blocks, block_len, heads_here, head_dim)
    q_blk = queries.reshape(shape)
    k_blk = keys.reshape(shape)
    v_blk = values.reshape(shape)
    block_state = jnp.einsum("nthd,nthe->nhde", k_blk, v_blk, preferred_element_type=jnp.float32)
    own_total = jnp.sum(block_state, axis=0)
    inside = jnp.cumsum(block_state, axis=0) - block_state
    zeros_state = jnp.zeros_like(own_total)
    before = prefix(own_total, "ctx", add_states, zeros_state)
    carried = (before[None] + inside).astype(jnp.bfloat16)
    causal = jnp.arange(block_len)[:, None] >= jnp.arange(block_len)[None, :]
    scores = jnp.einsum("nthd,nshd->nhts", q_blk, k_blk, preferred_element_type=jnp.float32)
    scores = jnp.where(causal[None, None], scores, 0.0).astype(jnp.bfloat16)
    intra = jnp.einsum("nhts,nshe->nthe", scores, v_blk, preferred_element_type=jnp.float32)
    inter = jnp.einsum("nthd,nhde->nthe", q_blk, carried, preferred_element_type=jnp.float32)
    attended = inter + intra
    normed = attended / jnp.sqrt(jnp.mean(attended * attended, axis=-1, keepdims=True) + 1e-06)
    normed = normed.astype(jnp.bfloat16).reshape(tok_rows, heads_here * head_dim)
    terms = jnp.dot(
        normed,
        lax.all_gather(out_weight, "ctx", axis=1, tiled=True),
        preferred_element_type=jnp.float32,
    )
    summed = lax.psum_scatter(terms.astype(jnp.bfloat16), "tp", scatter_dimension=0, tiled=True)
    return summed


def solution(mesh):
    placed = (P("ctx", "tp"), P("ctx", "tp"), P("ctx", "tp"), P("tp", "ctx"))
    return jax.shard_map(
        on_device, mesh=mesh, in_specs=placed, out_specs=P(("ctx", "tp"), None), check_vma=False
    )
```

profile of v0, /device:TPU:1, one launch (start us, length us, event | category | flops | bytes accessed | tf_op | source)
XLA Modules:
  0.0 274.9 jit_solution(6830236183896022547)
XLA Ops:
  6.5 0.0 copy-start
  6.5 0.0 all-gather.6.cloned.1.call-start
  6.5 1.3 copy.16
  7.9 1.3 copy.17
  9.1 1.0 fusion.14
  10.1 0.0 copy-start.1
  10.1 0.0 all-gather.6.cloned.1.call-update
  10.1 0.0 all-gather.4.cloned.1.call-start
  10.2 0.7 all-gather.4.cloned.1.call-update
  10.9 0.0 reduce-scatter.2.cloned.1.call-start
  10.9 0.1 iota_compare_fusion
  11.0 111.6 %all-gather.6.cloned.1.call-done = f32[256,128,128]{2,1,0:T(8,128)} async-done(((f32[4,128,128]{2,1,0:T(8,128)}), f32[256,128,128]{2,1,0:T(8,128)}) %all-gather.6.cloned.1.call-update) | async-done | bytes 16777232 | tf_op jit(solution)/shard_map/all_gather | solution.py:11
  122.6 1.0 while.10
  122.6 1.0 bitcast_add_fusion.2
  123.7 0.0 copy-done
  123.7 0.0 copy-done.1
  123.7 1.3 fusion.6
  125.0 2.6 multiply_reduce_fusion
  127.6 0.1 divide_convert_fusion
  127.7 79.9 %all-gather.4.cloned.1.call-done = bf16[512,4096]{0,1:T(8,128)(2,1)} async-done(((bf16[512,64]{0,1:T(8,128)(2,1)}), bf16[512,4096]{0,1:T(8,128)(2,1)}) %all-gather.4.cloned.1.call-update) | async-done | bytes 4194320 | tf_op jit(solution)/shard_map/all_gather | solution.py:50
  207.6 6.5 %convolution_convert_fusion = bf16[512,4096]{1,0:T(8,128)(2,1)} fusion(bf16[512,512]{0,1:T(8,128)(2,1)S(1)} %bitcast.44, bf16[512,4096]{0,1:T(8,128)(2,1)} %all-gather.4.cloned.1.call-done), kind=kOutput, calls=%fused_computation.1 | convolution fusion | flops 2149580800 | bytes 8912896 | tf_op jit(solution)/shard_map/dot_general | solution.py:48
  214.1 0.0 reduce-scatter.2.cloned.1.call-update
  214.1 54.2 %reduce-scatter.2.cloned.1.call-done = bf16[64,4096]{1,0:T(8,128)(2,1)} async-done(((bf16[512,4096]{1,0:T(8,128)(2,1)}), bf16[64,4096]{1,0:T(8,128)(2,1)}) %reduce-scatter.2.cloned.1.call-update) | async-done | bytes 524304 | tf_op jit(solution)/shard_map/reduce_scatter | solution.py:53
  (2 shorter events, 0.0 us)
Async XLA Ops:
  6.5 117.1 %copy-start = (bf16[512,512]{1,0:T(8,128)(2,1)S(1)}, bf16[512,512]{1,0:T(8,128)(2,1)}, u32[]{:S(2)}) copy-start(bf16[512,512]{1,0:T(8,128)(2,1)} %param.6) | copy-start | bytes 1572868
  6.5 116.1 %all-gather.6.cloned.1.call-start = ((), (), s32[]{:S(2)}) async-start(), calls=%async_computation.3 | async-start | bytes 17039360 | tf_op jit(solution)/shard_map/all_gather | solution.py:11
  10.1 113.6 %copy-start.1 = (f32[4,128,128]{2,1,0:T(8,128)S(1)}, f32[4,128,128]{2,1,0:T(8,128)}, u32[]{:S(2)}) copy-start(f32[4,128,128]{2,1,0:T(8,128)} %fusion.14) | copy-start | bytes 786436
  10.1 197.4 %all-gather.4.cloned.1.call-start = ((), (), s32[]{:S(2)}) async-start(), calls=%async_computation.1 | async-start | bytes 4259840 | tf_op jit(solution)/shard_map/all_gather | solution.py:50
  10.9 257.5 %reduce-scatter.2.cloned.1.call-start = ((), (), s32[]{:S(2)}) async-start(), calls=%async_computation.2 | async-start | bytes 4718592 | tf_op jit(solution)/shard_map/reduce_scatter | solution.py:53
Sparse Core Ops, SparseCore 0:
  10.7 111.8 all-gather.5
  125.9 81.5 all-gather.3
  214.3 54.0 reduce-scatter.1
where the time goes:
time: 277 us; the launch traced here: 275 us
  waiting for transfers between devices  246 us (89%)
  between operations  13.2 us (5%)
  matrix products  11.4 us (4%)
    all_gather x1, waiting for transfers between devices, prefix(): gathered = lax.all_gather(part, axis)  112 us
    all_gather x1, waiting for transfers between devices, on_device(): lax.all_gather(out_weight, 'ctx', axis=1, tiled=True)  79.9 us
    reduce_scatter x1, waiting for transfers between devices, on_device(): lax.psum_scatter(terms.astype(jnp.bfloat16), 'tp', scatter_dimension=0, t...  54.2 us
    dot_general x1, matrix products, on_device(): jnp.dot(normed, lax.all_gather(out_weight, 'ctx', axis=1, tiled=True), pr...  6.53 us
  transfers between devices with their start and end apart: 3, of which 3 were waited for; matrix products, arithmetic and copies ran while one was open for 2% of the time, Pallas kernels for 0%

commit v1 on v0

--- a/solution.py
+++ b/solution.py
@@ -4,6 +4,14 @@
 from jax.sharding import PartitionSpec as P
 
 HD = 128
+
+
+def gather_by_exchange(array, axis, dim):
+    count = lax.axis_size(axis)
+    repeats = [count if d == dim else 1 for d in range(array.ndim)]
+    return lax.all_to_all(
+        jnp.tile(array, repeats), axis, split_axis=dim, concat_axis=dim, tiled=True
+    )
 
 
 def prefix(part, axis, combine, identity):
@@ -46,9 +54,7 @@
     normed = attended / jnp.sqrt(jnp.mean(attended * attended, axis=-1, keepdims=True) + 1e-06)
     normed = normed.astype(jnp.bfloat16).reshape(tok_rows, heads_here * head_dim)
     terms = jnp.dot(
-        normed,
-        lax.all_gather(out_weight, "ctx", axis=1, tiled=True),
-        preferred_element_type=jnp.float32,
+        normed, gather_by_exchange(out_weight, "ctx", 1), preferred_element_type=jnp.float32
     )
     summed = lax.psum_scatter(terms.astype(jnp.bfloat16), "tp", scatter_dimension=0, tiled=True)
     return summed

time: 277 us -> 311 us (1.12)
  waiting for transfers between devices: 246 us -> 263 us
  starting transfers between devices: 0.08 us -> 15.1 us
    all_gather x1 -> x0, waiting for transfers between devices: 79.9 us -> none  [on_device(): lax.all_gather(out_weight, 'ctx', axis=1, tiled=True)]
    reduce_scatter x1, waiting for transfers between devices: 54.2 us -> 118 us  [on_device(): lax.psum_scatter(terms.astype(jnp.bfloat16), 'tp', scatter_dimension=0, t...]
    all_gather x1, waiting for transfers between devices: 112 us -> 145 us  [prefix(): gathered = lax.all_gather(part, axis)]
    all_to_all x0 -> x1, starting transfers between devices: none -> 15 us  [gather_by_exchange(): lax.all_to_all(jnp.tile(array, repeats), axis, split_axis=dim, concat_axi...]
    another operation x1 -> x2, local copies, waits for them, and re-layouts: 1.26 us -> 4.63 us  [the longest x1 3.32 us: gather_by_exchange(): jnp.tile(array, repeats)]
  transfers between devices with their start and end apart: 3 -> 3, of which waited for: 3 -> 2; matrix products, arithmetic and copies ran while one was open for 2% -> 2% of each run, Pallas kernels for 0% -> 0%
where the time goes in v1:
time: 311 us; the launch traced here: 309 us
  waiting for transfers between devices  263 us (85%)
  starting transfers between devices  15.1 us (5%)
  between operations  13.5 us (4%)
  matrix products  11.4 us (4%)
  local copies, waits for them, and re-layouts  4.66 us (1%)
    all_gather x1, waiting for transfers between devices, prefix(): gathered = lax.all_gather(part, axis)  145 us
    reduce_scatter x1, waiting for transfers between devices, on_device(): lax.psum_scatter(terms.astype(jnp.bfloat16), 'tp', scatter_dimension=0, t...  118 us
    all_to_all x1, starting transfers between devices, gather_by_exchange(): lax.all_to_all(jnp.tile(array, repeats), axis, split_axis=dim, concat_axi...  15 us
    dot_general x1, matrix products, on_device(): jnp.dot(normed, gather_by_exchange(out_weight, 'ctx', 1), preferred_eleme...  6.54 us
  transfers between devices with their start and end apart: 3, of which 2 were waited for; matrix products, arithmetic and copies ran while one was open for 2% of the time, Pallas kernels for 0%

profile of v1, /device:TPU:1, one launch (start us, length us, event | category | flops | bytes accessed | tf_op | source)
XLA Modules:
  0.0 309.2 jit_solution(3703349121056326130)
XLA Ops:
  6.5 0.0 copy-start
  6.5 0.0 all-gather.3.cloned.1.call-start
  6.5 1.3 copy.24
  7.9 2.1 fusion.8
  10.0 0.0 all-gather.3.cloned.1.call-update
  10.0 3.3 %tile.2 = bf16[512,64,64]{0,2,1:T(8,128)(2,1)} broadcast(bf16[512,64]{0,1:T(8,128)(2,1)} %param.9), dimensions={0,2} | broadcast | bytes 4259840 | tf_op jit(solution)/shard_map/tile | solution.py:13
  13.3 15.0 %all-to-all-start = ((bf16[512,64,64]{0,2,1:T(8,128)(2,1)}), bf16[512,64,64]{0,2,1:T(8,128)(2,1)}, u32[]{:S(2)}, u32[]{:S(2)}) async-start(bf16[512,64,64]{0,2,1:T(8,128)(2,1)} %tile.2), calls=%async_computation | async-start | bytes 8388608 | tf_op jit(solution)/shard_map/all_to_all | solution.py:12
  28.3 0.0 copy-start.1
  28.3 0.0 reduce-scatter.2.cloned.1.call-start
  28.4 0.1 iota_compare_fusion
  28.5 144.9 %all-gather.3.cloned.1.call-done = f32[256,128,128]{2,1,0:T(8,128)} async-done(((f32[4,128,128]{2,1,0:T(8,128)}), f32[256,128,128]{2,1,0:T(8,128)}) %all-gather.3.cloned.1.call-update) | async-done | bytes 16777232 | tf_op jit(solution)/shard_map/all_gather | solution.py:19
  173.4 1.0 while.10
  173.4 1.0 bitcast_add_fusion.2
  174.5 0.0 copy-done
  174.5 0.0 copy-done.1
  174.5 0.3 fusion.6
  174.8 2.4 multiply_reduce_fusion
  177.3 0.1 divide_convert_fusion
  177.4 0.0 all-to-all-done
  177.4 6.5 %convolution_convert_fusion = bf16[512,4096]{1,0:T(8,128)(2,1)} fusion(bf16[512,512]{0,1:T(8,128)(2,1)S(1)} %bitcast.56, bf16[512,4096]{0,1:T(8,128)(2,1)} %bitcast.7), kind=kOutput, calls=%fused_computation.1 | convolution fusion | flops 2149580800 | bytes 8912896 | tf_op jit(solution)/shard_map/dot_general | solution.py:56
  183.9 0.0 reduce-scatter.2.cloned.1.call-update
  184.0 118.4 %reduce-scatter.2.cloned.1.call-done = bf16[64,4096]{1,0:T(8,128)(2,1)} async-done(((bf16[512,4096]{1,0:T(8,128)(2,1)}), bf16[64,4096]{1,0:T(8,128)(2,1)}) %reduce-scatter.2.cloned.1.call-update) | async-done | bytes 524304 | tf_op jit(solution)/shard_map/reduce_scatter | solution.py:59
  (2 shorter events, 0.0 us)
Async XLA Ops:
  6.5 167.9 %copy-start = (bf16[512,512]{1,0:T(8,128)(2,1)S(1)}, bf16[512,512]{1,0:T(8,128)(2,1)}, u32[]{:S(2)}) copy-start(bf16[512,512]{1,0:T(8,128)(2,1)} %param.6) | copy-start | bytes 1572868
  6.5 166.8 %all-gather.3.cloned.1.call-start = ((), (), s32[]{:S(2)}) async-start(), calls=%async_computation.3 | async-start | bytes 17039360 | tf_op jit(solution)/shard_map/all_gather | solution.py:19
  13.3 164.1 %all-to-all-start = ((bf16[512,64,64]{0,2,1:T(8,128)(2,1)}), bf16[512,64,64]{0,2,1:T(8,128)(2,1)}, u32[]{:S(2)}, u32[]{:S(2)}) async-start(bf16[512,64,64]{0,2,1:T(8,128)(2,1)} %tile.2), calls=%async_computation | async-start | bytes 8388608 | tf_op jit(solution)/shard_map/all_to_all | solution.py:12
  28.3 146.1 %copy-start.1 = (f32[4,128,128]{2,1,0:T(8,128)S(1)}, f32[4,128,128]{2,1,0:T(8,128)}, u32[]{:S(2)}) copy-start(f32[4,128,128]{2,1,0:T(8,128)} %fusion.8) | copy-start | bytes 786436
  28.3 274.0 %reduce-scatter.2.cloned.1.call-start = ((), (), s32[]{:S(2)}) async-start(), calls=%async_computation.2 | async-start | bytes 4718592 | tf_op jit(solution)/shard_map/reduce_scatter | solution.py:59
Sparse Core Ops, SparseCore 0:
  10.7 162.6 all-gather.2
  184.1 118.2 reduce-scatter.1
